TPU v7x, 32 devices: a whole 2x2x4 slice. The times are simulated.
32 devices in a mesh: groups: 2 (over y), dp: 16 (over z, x, core).
Axes of the slice: x: 2, y: 2, z: 4, core: 2. Of those that a mesh axis runs over, the one named last changes fastest.
Arguments:
- hidden_acts: bfloat16 [32, 256, 16384], P(('groups', 'dp')), parts along dimension 0, as said below
- out_grads: bfloat16 [32, 256, 8192], P(('groups', 'dp')), parts along dimension 0, as said below
- proj_in: bfloat16 [64, 16384], P(None, 'dp'), may hold values from -0.046875 to 0.046875
- proj_out: bfloat16 [64, 8192], P(None, 'dp'), may hold values from -0.0625 to 0.0625
- lengths: int32 [32], P('groups'), parts along dimension 0, may hold values from 1 to 256, 2560 in all
- example_ids: int32 [32], P('groups'), parts along dimension 0, may hold values from 0 to 15, each once
Outputs:
- grad_store: float32 [32, 4096], P('groups', 'dp'), parts along dimension 0
- fisher_in: float32 [128, 64], P('groups'), parts along dimension 0
- fisher_out: float32 [128, 64], P('groups'), parts along dimension 0
There are 2 independent parts, one for each index of `groups`. A program takes and returns all parts, laid end to end along the dimension named above; an argument that names none is the same for every part. Nothing has to cross between parts.
Inputs may be any that keep to these rules, and one draw needn't show every extreme that they name: `lengths`: the longest sequence has all 256 positions. `example_ids`: each store row is named by exactly one sequence. `hidden_acts`: activations drawn with feature and sequence scales. `out_grads`: gradients drawn with feature and sequence scales.
All inputs are finite; a program needn't handle non-finite values.
Results may differ from a plain program's by a relative error of at most 0.0005.
Values may be sent and summed in bfloat16 or wider, within the bound.
A program may use at most 64 MiB of HBM per device.

v0:
```python
import math

import jax
import jax.numpy as jnp
from jax import lax
from jax.sharding import PartitionSpec as P


def local(hidden_acts, out_grads, proj_in, proj_out, lengths, example_ids):
    devices = lax.axis_size("dp")
    seq_block = lax.axis_index("dp")
    seq_count = hidden_acts.shape[0]
    local_len = hidden_acts.shape[1]
    rows = seq_count * local_len
    rank = proj_in.shape[0]
    in_cols = proj_in.shape[1]
    out_cols = proj_out.shape[1]
    total_seqs = example_ids.shape[0]
    flat_acts = hidden_acts.reshape(rows, in_cols * devices)
    flat_grads = out_grads.reshape(rows, out_cols * devices)
    joined = jnp.concatenate([proj_in, proj_out], axis=1)[None]
    gathered = lax.all_gather(joined, "dp", axis=0, tiled=True)
    in_side = jnp.einsum(
        "tnc,nrc->tr",
        flat_acts.reshape(rows, devices, in_cols),
        gathered[:, :, :in_cols],
        preferred_element_type=jnp.float32,
    )
    out_side = jnp.einsum(
        "tnc,nrc->tr",
        flat_grads.reshape(rows, devices, out_cols),
        gathered[:, :, in_cols:],
        preferred_element_type=jnp.float32,
    )
    first_seq = seq_block * seq_count
    my_lengths = lax.dynamic_slice_in_dim(lengths, first_seq, seq_count, 0)
    positions = jnp.arange(local_len, dtype=jnp.int32)
    live_mask = (positions[None, :] < my_lengths[:, None]).astype(jnp.float32)
    in_side = in_side.reshape(seq_count, local_len, rank)
    out_side = out_side.reshape(seq_count, local_len, rank)
    in_live = in_side * live_mask[:, :, None]
    out_live = out_side * live_mask[:, :, None]
    high = lax.Precision.HIGHEST
    example_terms = jnp.einsum("sci,scj->sij", out_live, in_side, precision=high).reshape(
        seq_count, rank * rank
    )
    factor_in = jnp.einsum("sci,scj->ij", in_live, in_side, precision=high)
    factor_out = jnp.einsum("sci,scj->ij", out_live, out_side, precision=high)
    count = jnp.sum(lengths).astype(jnp.float32)
    scale = 1.0 / math.sqrt(local_len)
    piece_width = rank * rank // devices
    outgoing = example_terms.reshape(seq_count, devices, piece_width)
    received = lax.all_to_all(outgoing, "dp", split_axis=1, concat_axis=0, tiled=True)
    received = received.reshape(total_seqs, piece_width)
    store_rows = jnp.arange(total_seqs, dtype=jnp.int32)
    routing_table = (store_rows[:, None] == example_ids[None, :]).astype(jnp.float32)
    store_part = jnp.dot(routing_table, received, precision=high)
    summed_in, summed_out = lax.psum((factor_in, factor_out), "dp")
    return (store_part * scale, summed_in / count, summed_out / count)


def solution(mesh):
    in_specs = (
        P(("groups", "dp"), None, None),
        P(("groups", "dp"), None, None),
        P(None, "dp"),
        P(None, "dp"),
        P("groups"),
        P("groups"),
    )
    out_specs = (P("groups", "dp"), P("groups", None), P("groups", None))
    return jax.shard_map(local, mesh=mesh, in_specs=in_specs, out_specs=out_specs, check_vma=False)
```

profile of v0, /device:TPU:0, one launch (start us, length us, event | category | flops | bytes accessed | tf_op | source)
XLA Modules:
  0.0 152.4 jit_solution(9327279756151381168)
XLA Ops:
  7.2 0.0 all-gather.3.cloned.1.call-start
  7.2 1.6 %pad_maximum_fusion = bf16[64,1536]{1,0:T(8,128)(2,1)} fusion(bf16[64,512]{1,0:T(8,128)(2,1)} %param.9, bf16[64,1024]{1,0:T(8,128)(2,1)} %param.8), kind=kLoop, calls=%fused_computation.9 | loop fusion | flops 393216 | bytes 393216 | tf_op jit(solution)/shard_map/concatenate | solution.py:21
  8.8 0.0 all-gather.3.cloned.1.call-update
  8.9 1.3 reduce_sum.9
  10.2 1.2 dynamic_slice.3
  11.4 15.3 %copy.16 = bf16[32,8,16,1024]{3,2,1,0:T(8,128)(2,1)} copy(bf16[32,8,16,1024]{3,1,2,0:T(8,128)(2,1)} %bitcast.18) | data formatting | bytes 16777216
  26.8 0.0 copy-done
  26.8 3.8 %copy.15 = bf16[32,8,16,512]{3,2,1,0:T(8,128)(2,1)} copy(bf16[32,8,16,512]{3,1,2,0:T(8,128)(2,1)S(1)} %bitcast.20) | data formatting | bytes 8388608
  31.2 0.7 compare_convert_fusion
  31.8 26.4 %all-gather.3.cloned.1.call-done = bf16[1024,1536]{1,0:T(8,128)(2,1)} async-done(((bf16[64,1536]{1,0:T(8,128)(2,1)}), bf16[1024,1536]{1,0:T(8,128)(2,1)}) %all-gather.3.cloned.1.call-update) | async-done | bytes 3145744 | tf_op jit(solution)/shard_map/all_gather | solution.py:22
  58.2 13.4 %fusion.8 = f32[64,256]{1,0:T(8,128)S(1)} fusion(bf16[256,16,1024]{2,1,0:T(8,128)(2,1)} %bitcast.19, bf16[16,64,1536]{2,1,0:T(8,128)(2,1)} %bitcast.22), kind=kOutput, calls=%fused_computation.6 | convolution fusion | flops 536870912 | bytes 10551296 | tf_op jit(solution)/shard_map/tnc,nrc->tr/dot_general | solution.py:23
  71.6 0.0 copy-start.2
  71.6 0.0 copy-done.1
  71.6 5.7 %fusion.5 = f32[64,256]{1,0:T(8,128)S(1)} fusion(bf16[256,16,512]{2,1,0:T(8,128)(2,1)S(1)} %bitcast.21, bf16[16,64,1536]{2,1,0:T(8,128)(2,1)} %bitcast.23), kind=kOutput, calls=%fused_computation.5 | convolution fusion | flops 268435456 | bytes 5308416 | tf_op jit(solution)/shard_map/tnc,nrc->tr/dot_general | solution.py:29
  77.4 0.2 fusion.14
  77.6 0.2 fusion.16
  77.8 0.2 fusion.18
  78.0 0.7 reshape_reshape.12
  78.7 3.5 %all-to-all-start = ((f32[1,16,256]{2,0,1:T(1,128)}), f32[1,16,256]{2,0,1:T(1,128)S(1)}, u32[]{:S(2)}, u32[]{:S(2)}) async-start(f32[1,16,256]{2,0,1:T(1,128)} %reshape_reshape.12), calls=%async_computation | async-start | bytes 32768 | tf_op jit(solution)/shard_map/all_to_all | solution.py:53
  82.2 62.0 %all-reduce = (f32[64,64]{1,0:T(8,128)S(1)}, f32[64,64]{1,0:T(8,128)S(1)}) all-reduce(f32[64,64]{1,0:T(8,128)S(1)} %fusion.14, f32[64,64]{1,0:T(8,128)S(1)} %fusion.16), channel_id=1, replica_groups=mesh['groups'=2,'dp'=16] {'dp'}, use_global_device_ids=true, to_apply=%region_0.0 | all-reduce | flops 8192 | bytes 65536 | tf_op jit(solution)/shard_map/psum | solution.py:58
  144.2 0.6 broadcast_divide_fusion
  144.8 0.0 all-to-all-done
  144.8 0.0 copy-done.2
  144.8 0.7 convolution_multiply_fusion
  (2 shorter events, 0.0 us)
Async XLA Ops:
  7.2 51.0 %all-gather.3.cloned.1.call-start = ((), (), s32[]{:S(2)}) async-start(), calls=%async_computation.1 | async-start | bytes 3342336 | tf_op jit(solution)/shard_map/all_gather | solution.py:22
  11.4 15.4 %copy-start = (bf16[1,256,8192]{2,1,0:T(8,128)(2,1)S(1)}, bf16[1,256,8192]{2,1,0:T(8,128)(2,1)}, u32[]{:S(2)}) copy-start(bf16[1,256,8192]{2,1,0:T(8,128)(2,1)} %param.7) | copy-start | bytes 12582916
  58.2 13.4 %copy-start.1 = (bf16[32,8,16,512]{3,2,1,0:T(8,128)(2,1)S(1)}, bf16[32,8,16,512]{3,2,1,0:T(8,128)(2,1)}, u32[]{:S(2)}) copy-start(bf16[32,8,16,512]{3,2,1,0:T(8,128)(2,1)} %copy.15) | copy-start | bytes 12582916
  71.6 73.2 %copy-start.2 = (s32[16]{0:T(128)S(1)}, s32[16]{0:T(128)}, u32[]{:S(2)}) copy-start(s32[16]{0:T(128)} %param.11) | copy-start | bytes 196
  78.7 66.1 %all-to-all-start = ((f32[1,16,256]{2,0,1:T(1,128)}), f32[1,16,256]{2,0,1:T(1,128)S(1)}, u32[]{:S(2)}, u32[]{:S(2)}) async-start(f32[1,16,256]{2,0,1:T(1,128)} %reshape_reshape.12), calls=%async_computation | async-start | bytes 32768 | tf_op jit(solution)/shard_map/all_to_all | solution.py:53
Sparse Core Ops, SparseCore 0:
  10.3 47.8 all-gather.2
where the time goes:
time: 153 us; the launch traced here: 152 us
  blocking collectives  62 us (41%)
  waiting for transfers between devices  26.4 us (17%)
  local copies, waits for them, and re-layouts  21.1 us (14%)
  matrix products  20.5 us (13%)
  between operations  14.8 us (10%)
  other arithmetic  4.21 us (3%)
  starting transfers between devices  3.55 us (2%)
    psum x1, blocking collectives, local(): summed_in, summed_out = lax.psum((factor_in, factor_out), 'dp')  62 us
    all_gather x1, waiting for transfers between devices, local(): gathered = lax.all_gather(joined, 'dp', axis=0, tiled=True)  26.4 us
    unnamed x8, local copies, waits for them, and re-layouts  19.1 us
    dot_general x1, matrix products, local(): jnp.einsum('tnc,nrc->tr', flat_acts.reshape(rows, devices, in_cols), gath...  13.4 us
    dot_general x1, matrix products, local(): jnp.einsum('tnc,nrc->tr', flat_grads.reshape(rows, devices, out_cols), ga...  5.73 us
    all_to_all x1, starting transfers between devices, local(): lax.all_to_all(outgoing, 'dp', split_axis=1, concat_axis=0, tiled=True)  3.52 us
  transfers between devices with their start and end apart: 2, of which 1 were waited for; matrix products, arithmetic and copies ran while one was open for 15% of the time, Pallas kernels for 0%

commit v1 on v0

--- a/solution.py
+++ b/solution.py
@@ -1,9 +1,226 @@
+import functools
 import math
 
 import jax
 import jax.numpy as jnp
 from jax import lax
+from jax.experimental import pallas as pl
+from jax.experimental.pallas import tpu as pltpu
 from jax.sharding import PartitionSpec as P
+
+KEYS = ((0, 0), (0, 1), (1, 0), (2, 0), (3, 0), (1, 1), (2, 1), (3, 1))
+MESH = pl.DeviceIdType.MESH
+
+
+def kernel(
+    scale,
+    acts_hbm, grads_hbm, pin_hbm, pout_hbm, lengths, ids,
+    store_ref, fin_ref, fout_ref,
+    acts, grads, gin, gout, acc_in, acc_out, slabs, terms, piece, totals,
+    acts_sem, grads_sem, own_sem, send_sem, in_sem, out_sem,
+    term_send, term_sem, tot_send, tot_sem,
+):
+    y = lax.axis_index("groups")
+    me = lax.axis_index("dp")
+    z, x, c = me // 4, (me // 2) % 2, me % 2
+    devices = gin.shape[0]
+    in_cols, out_cols = gin.shape[2], gout.shape[2]
+    rank = fin_ref.shape[0]
+    rows = rank // devices
+    is_main = c == y
+
+    def index(key, core):
+        k, other = key
+        return (z ^ k) * 4 + (x ^ other) * 2 + core
+
+    order = [(KEYS[0], 0)]
+    for i in range(1, len(KEYS)):
+        order += [(KEYS[i], 0), (KEYS[i - 1], 1)]
+    order.append((KEYS[-1], 1))
+    pieces = [index(key, c ^ s) for key, s in order]
+
+    own_in = pltpu.make_async_copy(pin_hbm, gin.at[me], own_sem.at[0])
+    own_out = pltpu.make_async_copy(pout_hbm, gout.at[me], own_sem.at[1])
+    own_in.start()
+    own_out.start()
+    barrier = pltpu.get_barrier_semaphore()
+    for d in range(1, devices):
+        pl.semaphore_signal(barrier, inc=1, device_id=(y, me ^ d), device_id_type=MESH)
+    pl.semaphore_signal(barrier, inc=1, device_id=(1 - y, me), device_id_type=MESH)
+    loads = []
+    for n, p in enumerate(pieces):
+        a = pltpu.make_async_copy(
+            acts_hbm.at[:, pl.ds(pl.multiple_of(p * in_cols, in_cols), in_cols)],
+            acts.at[n], acts_sem.at[n])
+        b = pltpu.make_async_copy(
+            grads_hbm.at[:, pl.ds(pl.multiple_of(p * out_cols, out_cols), out_cols)],
+            grads.at[n], grads_sem.at[n])
+        a.start()
+        b.start()
+        loads.append((a, b))
+    own_in.wait()
+    own_out.wait()
+    pl.semaphore_wait(barrier, devices)
+
+    sends = []
+
+    def send(p, target, when=None):
+        slot = len(sends)
+        both = [
+            pltpu.make_async_remote_copy(
+                src_ref=buf.at[p], dst_ref=buf.at[p], send_sem=send_sem.at[j, slot],
+                recv_sem=sem.at[p], device_id=target, device_id_type=MESH)
+            for j, (buf, sem) in enumerate(((gin, in_sem), (gout, out_sem)))
+        ]
+        sends.append((both, when))
+        if when is None:
+            for copy in both:
+                copy.start()
+        else:
+            @pl.when(when)
+            def _():
+                for copy in both:
+                    copy.start()
+
+    def arrived(p):
+        for buf, sem in ((gin, in_sem), (gout, out_sem)):
+            pltpu.make_async_copy(buf.at[p], buf.at[p], sem.at[p]).wait()
+
+    across = (y, me ^ 2)
+    sibling = (y, me ^ 1)
+    opposite = (1 - y, me)
+
+    def forward(key):
+        p = index(key, c)
+        k, other = key
+        if other == 0:
+            if k == 0:
+                for d in (1, 3, 2):
+                    send(p, (y, me ^ (4 * d)), is_main)
+                send(p, across)
+            else:
+                send(p, opposite, is_main)
+                send(p, across, None if k == 3 else is_main)
+        elif k in (1, 2):
+            send(p, opposite, is_main)
+        send(p, sibling)
+
+    acc_in[...] = jnp.zeros_like(acc_in)
+    acc_out[...] = jnp.zeros_like(acc_out)
+    for n, ((key, s), p) in enumerate(zip(order, pieces)):
+        if n:
+            arrived(p)
+        if s == 0:
+            forward(key)
+        for copy in loads[n]:
+            copy.wait()
+        for acc, buf, g in ((acc_in, acts, gin), (acc_out, grads, gout)):
+            acc[...] += lax.dot_general(
+                buf[n], g[p], (((1,), (1,)), ((), ())),
+                preferred_element_type=jnp.float32)
+
+    both = jnp.concatenate([acc_in[...], acc_out[...]], axis=1)
+    position = lax.broadcasted_iota(jnp.int32, both.shape, 0)
+    live = jnp.where(position < lengths[me], both, 0.0)
+    gram = lax.dot_general(
+        live, both, (((0,), (0,)), ((), ())),
+        precision=lax.Precision.HIGHEST, preferred_element_type=jnp.float32)
+    for d in range(devices):
+        slabs[d, 0:rows, :] = gram[d * rows:(d + 1) * rows, :]
+        slabs[d, rows:2 * rows, :] = gram[rank + d * rows:rank + (d + 1) * rows, :]
+    copies = []
+    for d in range(1, devices):
+        q = me ^ d
+        copy = pltpu.make_async_remote_copy(
+            src_ref=slabs.at[q], dst_ref=terms.at[me], send_sem=term_send.at[d],
+            recv_sem=term_sem.at[me], device_id=(y, q), device_id_type=MESH)
+        copy.start()
+        copies.append(copy)
+    terms[me] = slabs[me]
+    count = lengths[0]
+    for d in range(1, lengths.shape[0]):
+        count = count + lengths[d]
+    for d in range(1, devices):
+        q = me ^ d
+        pltpu.make_async_copy(slabs.at[q], terms.at[q], term_sem.at[q]).wait()
+    total = terms[0]
+    for d in range(1, devices):
+        total = total + terms[d]
+    total = total / jnp.full(total.shape, count.astype(jnp.float32))
+    piece[...] = total
+    for d in range(1, devices):
+        copy = pltpu.make_async_remote_copy(
+            src_ref=piece, dst_ref=totals.at[me], send_sem=tot_send.at[d],
+            recv_sem=tot_sem.at[me], device_id=(y, me ^ d), device_id_type=MESH)
+        copy.start()
+        copies.append(copy)
+    totals[me] = total
+    row = lax.broadcasted_iota(jnp.int32, store_ref.shape, 0)
+    store = jnp.zeros(store_ref.shape, jnp.float32)
+    for d in range(devices):
+        store = store + jnp.where(row == ids[d], terms[d, rows:2 * rows, :][None], 0.0)
+    store_ref[...] = store * scale
+    for d in range(1, devices):
+        q = me ^ d
+        pltpu.make_async_copy(piece, totals.at[q], tot_sem.at[q]).wait()
+    for d in range(devices):
+        fin_ref[d * rows:(d + 1) * rows, :] = totals[d, 0:rows, 0:rank]
+        fout_ref[d * rows:(d + 1) * rows, :] = totals[d, rows:2 * rows, rank:2 * rank]
+    for copy in copies:
+        copy.wait_send()
+    for pair, when in sends:
+        if when is None:
+            for copy in pair:
+                copy.wait_send()
+        else:
+            @pl.when(when)
+            def _():
+                for copy in pair:
+                    copy.wait_send()
+
+
+def fused(hidden_acts, out_grads, proj_in, proj_out, lengths, example_ids):
+    devices = lax.axis_size("dp")
+    length, ffw = hidden_acts.shape[1:]
+    width = out_grads.shape[2]
+    rank, in_cols = proj_in.shape
+    out_cols = proj_out.shape[1]
+    rows = rank // devices
+    f32, bf16 = jnp.float32, jnp.bfloat16
+    dma = pltpu.SemaphoreType.DMA
+    store, fin, fout = pl.pallas_call(
+        functools.partial(kernel, 1.0 / math.sqrt(length)),
+        out_shape=(
+            jax.ShapeDtypeStruct((devices, rows, 2 * rank), f32),
+            jax.ShapeDtypeStruct((rank, rank), f32),
+            jax.ShapeDtypeStruct((rank, rank), f32),
+        ),
+        in_specs=[pl.BlockSpec(memory_space=pl.ANY)] * 4
+        + [pl.BlockSpec(memory_space=pltpu.SMEM)] * 2,
+        out_specs=[pl.BlockSpec(memory_space=pltpu.VMEM)] * 3,
+        scratch_shapes=[
+            pltpu.VMEM((devices, length, in_cols), bf16),
+            pltpu.VMEM((devices, length, out_cols), bf16),
+            pltpu.VMEM((devices, rank, in_cols), bf16),
+            pltpu.VMEM((devices, rank, out_cols), bf16),
+            pltpu.VMEM((length, rank), f32),
+            pltpu.VMEM((length, rank), f32),
+            pltpu.VMEM((devices, 2 * rows, 2 * rank), f32),
+            pltpu.VMEM((devices, 2 * rows, 2 * rank), f32),
+            pltpu.VMEM((2 * rows, 2 * rank), f32),
+            pltpu.VMEM((devices, 2 * rows, 2 * rank), f32),
+            dma((devices,)), dma((devices,)), dma((2,)), dma((2, 24)),
+            dma((devices,)), dma((devices,)),
+            dma((devices,)), dma((devices,)), dma((devices,)), dma((devices,)),
+        ],
+        compiler_params=pltpu.CompilerParams(
+            collective_id=0, has_side_effects=True, vmem_limit_bytes=40 * 1024 * 1024),
+        cost_estimate=pl.CostEstimate(
+            flops=2 * length * rank * (ffw + width),
+            bytes_accessed=2 * length * (ffw + width), transcendentals=0),
+    )(hidden_acts.reshape(length, ffw), out_grads.reshape(length, width),
+      proj_in, proj_out, lengths, example_ids)
+    return store[:, :, :rank].reshape(devices, rows * rank), fin, fout
 
 
 def local(hidden_acts, out_grads, proj_in, proj_out, lengths, example_ids):
@@ -69,4 +286,9 @@
         P("groups"),
     )
     out_specs = (P("groups", "dp"), P("groups", None), P("groups", None))
-    return jax.shard_map(local, mesh=mesh, in_specs=in_specs, out_specs=out_specs, check_vma=False)
+    fits = mesh.shape["groups"] == 2 and mesh.shape["dp"] == 16
+
+    def body(*args):
+        return (fused if fits and args[0].shape[0] == 1 else local)(*args)
+
+    return jax.shard_map(body, mesh=mesh, in_specs=in_specs, out_specs=out_specs, check_vma=False)

time: 153 us -> 54.2 us (0.35)
  blocking collectives: 62 us -> 0 us
  Pallas kernels: 0 us -> 42.7 us
  waiting for transfers between devices: 26.4 us -> 0 us
  matrix products: 20.5 us -> 0 us
  between operations: 14.8 us -> 0.65 us
  local copies, waits for them, and re-layouts: 21.1 us -> 10.5 us
  other arithmetic: 4.21 us -> 0 us
  starting transfers between devices: 3.55 us -> 0 us
    psum x1 -> x0, blocking collectives: 62 us -> none  [local(): summed_in, summed_out = lax.psum((factor_in, factor_out), 'dp')]
    pallas_call x0 -> x1, Pallas kernels: none -> 42.7 us  [fused(): pl.pallas_call(functools.partial(kernel, 1.0 / math.sqrt(length)), out_sh...]
    all_gather x1 -> x0, waiting for transfers between devices: 26.4 us -> none  [local(): gathered = lax.all_gather(joined, 'dp', axis=0, tiled=True)]
    dot_general x6 -> x0, matrix products: 20.5 us -> none  [the longest x1 13.4 us: local(): jnp.einsum('tnc,nrc->tr', flat_acts.reshape(rows, devices, in_cols), gath...]
    unnamed x8 -> x14, local copies, waits for them, and re-layouts: 19.1 us -> 9.84 us
    all_to_all x1 -> x0, starting transfers between devices: 3.52 us -> none  [local(): lax.all_to_all(outgoing, 'dp', split_axis=1, concat_axis=0, tiled=True)]
    concatenate x1 -> x0, other arithmetic: 1.63 us -> none  [local(): joined = jnp.concatenate([proj_in, proj_out], axis=1)[None]]
  transfers between devices with their start and end apart: 2 -> 0, of which waited for: 1 -> 0; matrix products, arithmetic and copies ran while one was open for 15% -> 0% of each run, Pallas kernels for 0% -> 0%
where the time goes in v1:
time: 54.2 us; the launch traced here: 53.9 us
  Pallas kernels  42.7 us (79%)
  local copies, waits for them, and re-layouts  10.5 us (19%)
  between operations  0.65 us (1%)
    pallas_call x1, Pallas kernels, fused(): pl.pallas_call(functools.partial(kernel, 1.0 / math.sqrt(length)), out_sh...  42.7 us
    unnamed x14, local copies, waits for them, and re-layouts  9.84 us

profile of v1, /device:TPU:0, one launch (start us, length us, event | category | flops | bytes accessed | tf_op | source)
XLA Modules:
  0.0 53.9 jit_solution(459145276662689464)
XLA Ops:
  0.6 0.0 copy-start
  0.6 3.4 %copy-done = bf16[1,256,16384]{2,1,0:T(8,128)(2,1)S(1)} copy-done((bf16[1,256,16384]{2,1,0:T(8,128)(2,1)S(1)}, bf16[1,256,16384]{2,1,0:T(8,128)(2,1)}, u32[]{:S(2)}) %copy-start) | copy-done | bytes 8388632
  4.0 0.0 copy-start.1
  4.0 2.2 %copy-done.1 = bf16[1,256,8192]{2,1,0:T(8,128)(2,1)S(1)} copy-done((bf16[1,256,8192]{2,1,0:T(8,128)(2,1)S(1)}, bf16[1,256,8192]{2,1,0:T(8,128)(2,1)}, u32[]{:S(2)}) %copy-start.1) | copy-done | bytes 4194328
  6.2 0.0 copy-start.2
  6.2 0.9 %copy-done.2 = bf16[64,1024]{1,0:T(8,128)(2,1)S(1)} copy-done((bf16[64,1024]{1,0:T(8,128)(2,1)S(1)}, bf16[64,1024]{1,0:T(8,128)(2,1)}, u32[]{:S(2)}) %copy-start.2) | copy-done | bytes 131096
  7.1 0.0 copy-start.3
  7.1 0.8 %copy-done.3 = bf16[64,512]{1,0:T(8,128)(2,1)S(1)} copy-done((bf16[64,512]{1,0:T(8,128)(2,1)S(1)}, bf16[64,512]{1,0:T(8,128)(2,1)}, u32[]{:S(2)}) %copy-start.3) | copy-done | bytes 65560
  7.9 0.0 copy-start.4
  8.0 0.7 %copy-done.4 = s32[16]{0:T(128)S(1)} copy-done((s32[16]{0:T(128)S(1)}, s32[16]{0:T(128)}, u32[]{:S(2)}) %copy-start.4) | copy-done | bytes 88
  8.6 0.0 copy-start.5
  8.6 0.7 %copy-done.5 = s32[16]{0:T(128)S(1)} copy-done((s32[16]{0:T(128)S(1)}, s32[16]{0:T(128)}, u32[]{:S(2)}) %copy-start.5) | copy-done | bytes 88
  9.3 42.7 %shard_map.85 = (f32[16,4,128]{2,1,0:T(4,128)S(1)}, f32[64,64]{1,0:T(8,128)S(1)}, f32[64,64]{1,0:T(8,128)S(1)}) custom-call(bf16[256,16384]{1,0:T(8,128)(2,1)S(1)} %bitcast.3, bf16[256,8192]{1,0:T(8,128)(2,1)S(1)} %bitcast.4, bf16[64,1024]{1,0:T(8,128)(2,1)S(1)} %copy-done.2, bf16[64,512]{1,0:T(8,128)(2,1)S(1)} %copy-done.3, s32[16]{0:T(128)S(1)} %copy-done.4, ...), custom_call_target="tpu_custom_call" | custom-call | flops 805306368 | bytes 12582912 | tf_op jit(solution)/shard_map/pallas_call | solution.py:191
  52.0 0.7 %reshape.17 = f32[16,256]{1,0:T(8,128)} reshape(f32[16,4,64]{2,1,0:T(4,128)S(1)} %bitcast.5) | data formatting | bytes 32768 | tf_op jit(solution)/shard_map/reshape | solution.py:223
  52.7 0.6 %copy.11 = f32[64,64]{1,0:T(8,128)} copy(f32[64,64]{1,0:T(8,128)S(1)} %get-tuple-element.13) | data formatting | bytes 32768
  53.3 0.6 %copy.12 = f32[64,64]{1,0:T(8,128)} copy(f32[64,64]{1,0:T(8,128)S(1)} %get-tuple-element.14) | data formatting | bytes 32768
Async XLA Ops:
  0.6 3.4 %copy-start = (bf16[1,256,16384]{2,1,0:T(8,128)(2,1)S(1)}, bf16[1,256,16384]{2,1,0:T(8,128)(2,1)}, u32[]{:S(2)}) copy-start(bf16[1,256,16384]{2,1,0:T(8,128)(2,1)} %param.6) | copy-start | bytes 25165828
  4.0 2.2 %copy-start.1 = (bf16[1,256,8192]{2,1,0:T(8,128)(2,1)S(1)}, bf16[1,256,8192]{2,1,0:T(8,128)(2,1)}, u32[]{:S(2)}) copy-start(bf16[1,256,8192]{2,1,0:T(8,128)(2,1)} %param.7) | copy-start | bytes 12582916
  6.2 0.9 %copy-start.2 = (bf16[64,1024]{1,0:T(8,128)(2,1)S(1)}, bf16[64,1024]{1,0:T(8,128)(2,1)}, u32[]{:S(2)}) copy-start(bf16[64,1024]{1,0:T(8,128)(2,1)} %pin_hbm.1) | copy-start | bytes 393220
  7.1 0.8 %copy-start.3 = (bf16[64,512]{1,0:T(8,128)(2,1)S(1)}, bf16[64,512]{1,0:T(8,128)(2,1)}, u32[]{:S(2)}) copy-start(bf16[64,512]{1,0:T(8,128)(2,1)} %pout_hbm.1) | copy-start | bytes 196612
  7.9 0.7 %copy-start.4 = (s32[16]{0:T(128)S(1)}, s32[16]{0:T(128)}, u32[]{:S(2)}) copy-start(s32[16]{0:T(128)} %lengths.1) | copy-start | bytes 196
  8.6 0.7 %copy-start.5 = (s32[16]{0:T(128)S(1)}, s32[16]{0:T(128)}, u32[]{:S(2)}) copy-start(s32[16]{0:T(128)} %ids.1) | copy-start | bytes 196

commit v2 on v1

--- a/solution.py
+++ b/solution.py
@@ -8,7 +8,9 @@
 from jax.experimental.pallas import tpu as pltpu
 from jax.sharding import PartitionSpec as P
 
-KEYS = ((0, 0), (0, 1), (1, 0), (2, 0), (3, 0), (1, 1), (2, 1), (3, 1))
+KEYS = ((0, 0), (1, 0), (0, 1), (2, 0), (1, 1), (3, 0), (2, 1), (3, 1))
+LAG = 4
+CHUNKS = 3
 MESH = pl.DeviceIdType.MESH
 
 
@@ -16,9 +18,9 @@
     scale,
     acts_hbm, grads_hbm, pin_hbm, pout_hbm, lengths, ids,
     store_ref, fin_ref, fout_ref,
-    acts, grads, gin, gout, acc_in, acc_out, slabs, terms, piece, totals,
-    acts_sem, grads_sem, own_sem, send_sem, in_sem, out_sem,
-    term_send, term_sem, tot_send, tot_sem,
+    acts, grads, gin, gout, acc_in, acc_out, slabs, terms, examples, grads_in, piece, totals,
+    acts_sem, grads_sem, own_sem, send_sem, in_sem,
+    term_send, term_sem, example_send, example_sem, tot_send, tot_sem,
 ):
     y = lax.axis_index("groups")
     me = lax.axis_index("dp")
@@ -29,14 +31,19 @@
     rows = rank // devices
     is_main = c == y
 
+    inner = jnp.logical_or(z == 1, z == 2)
+    planes = (z, z ^ 1, z ^ jnp.where(inner, 3, 2), z ^ jnp.where(inner, 2, 3))
+
     def index(key, core):
-        k, other = key
-        return (z ^ k) * 4 + (x ^ other) * 2 + core
-
-    order = [(KEYS[0], 0)]
-    for i in range(1, len(KEYS)):
-        order += [(KEYS[i], 0), (KEYS[i - 1], 1)]
-    order.append((KEYS[-1], 1))
+        step, other = key
+        return planes[step] * 4 + (x ^ other) * 2 + core
+
+    order = []
+    for i in range(len(KEYS) + LAG):
+        if i < len(KEYS):
+            order.append((KEYS[i], 0))
+        if i >= LAG:
+            order.append((KEYS[i - LAG], 1))
     pieces = [index(key, c ^ s) for key, s in order]
 
     own_in = pltpu.make_async_copy(pin_hbm, gin.at[me], own_sem.at[0])
@@ -44,8 +51,17 @@
     own_in.start()
     own_out.start()
     barrier = pltpu.get_barrier_semaphore()
-    for d in range(1, devices):
+    for d in (1, 2):
         pl.semaphore_signal(barrier, inc=1, device_id=(y, me ^ d), device_id_type=MESH)
+
+    @pl.when(z < 3)
+    def _():
+        pl.semaphore_signal(barrier, inc=1, device_id=(y, me + 4), device_id_type=MESH)
+
+    @pl.when(z > 0)
+    def _():
+        pl.semaphore_signal(barrier, inc=1, device_id=(y, me - 4), device_id_type=MESH)
+
     pl.semaphore_signal(barrier, inc=1, device_id=(1 - y, me), device_id_type=MESH)
     loads = []
     for n, p in enumerate(pieces):
@@ -60,58 +76,64 @@
         loads.append((a, b))
     own_in.wait()
     own_out.wait()
-    pl.semaphore_wait(barrier, devices)
+    pl.semaphore_wait(barrier, 3 + (z < 3).astype(jnp.int32) + (z > 0).astype(jnp.int32))
 
     sends = []
 
-    def send(p, target, when=None):
+    def chunk(j, p):
+        if j == 2:
+            return gout.at[p]
+        half = rank // 2
+        return gin.at[p, pl.ds(j * half, half), :]
+
+    def send(j, p, target, when=None):
         slot = len(sends)
-        both = [
-            pltpu.make_async_remote_copy(
-                src_ref=buf.at[p], dst_ref=buf.at[p], send_sem=send_sem.at[j, slot],
-                recv_sem=sem.at[p], device_id=target, device_id_type=MESH)
-            for j, (buf, sem) in enumerate(((gin, in_sem), (gout, out_sem)))
-        ]
-        sends.append((both, when))
+        copy = pltpu.make_async_remote_copy(
+            src_ref=chunk(j, p), dst_ref=chunk(j, p), send_sem=send_sem.at[slot],
+            recv_sem=in_sem.at[j, p], device_id=target, device_id_type=MESH)
+        sends.append((copy, when))
         if when is None:
-            for copy in both:
-                copy.start()
+            copy.start()
         else:
-            @pl.when(when)
-            def _():
-                for copy in both:
-                    copy.start()
-
-    def arrived(p):
-        for buf, sem in ((gin, in_sem), (gout, out_sem)):
-            pltpu.make_async_copy(buf.at[p], buf.at[p], sem.at[p]).wait()
+            pl.when(when)(copy.start)
+
+    def arrived(j, p):
+        pltpu.make_async_copy(chunk(j, p), chunk(j, p), in_sem.at[j, p]).wait()
 
     across = (y, me ^ 2)
     sibling = (y, me ^ 1)
     opposite = (1 - y, me)
 
-    def forward(key):
+    def forward(j, key):
         p = index(key, c)
-        k, other = key
+        step, other = key
         if other == 0:
-            if k == 0:
-                for d in (1, 3, 2):
-                    send(p, (y, me ^ (4 * d)), is_main)
-                send(p, across)
+            line = jnp.logical_or(is_main, j == 2)
+            plane = planes[step]
+            up = jnp.logical_and(plane <= z, z < 3)
+            down = jnp.logical_and(plane >= z, z > 0)
+            if step == 0:
+                send(j, p, (y, jnp.where(up, me + 4, me)), jnp.logical_and(line, up))
+                send(j, p, (y, jnp.where(down, me - 4, me)), jnp.logical_and(line, down))
+                send(j, p, across)
             else:
-                send(p, opposite, is_main)
-                send(p, across, None if k == 3 else is_main)
-        elif k in (1, 2):
-            send(p, opposite, is_main)
-        send(p, sibling)
+                send(j, p, (y, jnp.where(up, me + 4, jnp.where(down, me - 4, me))),
+                     jnp.logical_and(line, jnp.logical_or(up, down)))
+                send(j, p, across, is_main)
+                if j < 2:
+                    send(j, p, opposite, is_main)
+        elif step:
+            send(j, p, opposite, is_main)
+        send(j, p, sibling)
 
     acc_in[...] = jnp.zeros_like(acc_in)
     acc_out[...] = jnp.zeros_like(acc_out)
     for n, ((key, s), p) in enumerate(zip(order, pieces)):
-        if n:
-            arrived(p)
-        if s == 0:
-            forward(key)
+        for j in range(CHUNKS):
+            if n:
+                arrived(j, p)
+            if s == 0:
+                forward(j, key)
         for copy in loads[n]:
             copy.wait()
         for acc, buf, g in ((acc_in, acts, gin), (acc_out, grads, gout)):
@@ -125,58 +147,70 @@
     gram = lax.dot_general(
         live, both, (((0,), (0,)), ((), ())),
         precision=lax.Precision.HIGHEST, preferred_element_type=jnp.float32)
+    lane = lax.broadcasted_iota(jnp.int32, (rank, 2 * rank), 1)
+    factors = jnp.where(lane < rank, gram[:rank, :], gram[rank:, :])
+    copies = []
+
+    def scatter(slabs, terms, sends, arrivals):
+        for d in reversed(range(1, devices)):
+            q = me ^ d
+            copy = pltpu.make_async_remote_copy(
+                src_ref=slabs.at[q], dst_ref=terms.at[me], send_sem=sends.at[d],
+                recv_sem=arrivals.at[me], device_id=(y, q), device_id_type=MESH)
+            copy.start()
+            copies.append(copy)
+        terms[me] = slabs[me]
+
+    def collect(terms, arrivals):
+        for d in range(1, devices):
+            q = me ^ d
+            pltpu.make_async_copy(terms.at[q], terms.at[q], arrivals.at[q]).wait()
+
     for d in range(devices):
-        slabs[d, 0:rows, :] = gram[d * rows:(d + 1) * rows, :]
-        slabs[d, rows:2 * rows, :] = gram[rank + d * rows:rank + (d + 1) * rows, :]
-    copies = []
-    for d in range(1, devices):
-        q = me ^ d
-        copy = pltpu.make_async_remote_copy(
-            src_ref=slabs.at[q], dst_ref=terms.at[me], send_sem=term_send.at[d],
-            recv_sem=term_sem.at[me], device_id=(y, q), device_id_type=MESH)
-        copy.start()
-        copies.append(copy)
-    terms[me] = slabs[me]
+        slabs[d] = factors[d * rows:(d + 1) * rows, :]
+    scatter(slabs, terms, term_send, term_sem)
+    for d in range(devices):
+        examples[d] = gram[rank + d * rows:rank + (d + 1) * rows, :]
+    scatter(examples, grads_in, example_send, example_sem)
     count = lengths[0]
     for d in range(1, lengths.shape[0]):
         count = count + lengths[d]
-    for d in range(1, devices):
-        q = me ^ d
-        pltpu.make_async_copy(slabs.at[q], terms.at[q], term_sem.at[q]).wait()
-    total = terms[0]
-    for d in range(1, devices):
-        total = total + terms[d]
+    collect(terms, term_sem)
+    total = jnp.sum(terms[...], axis=0)
     total = total / jnp.full(total.shape, count.astype(jnp.float32))
     piece[...] = total
-    for d in range(1, devices):
+    for d in reversed(range(1, devices)):
         copy = pltpu.make_async_remote_copy(
             src_ref=piece, dst_ref=totals.at[me], send_sem=tot_send.at[d],
             recv_sem=tot_sem.at[me], device_id=(y, me ^ d), device_id_type=MESH)
         copy.start()
         copies.append(copy)
     totals[me] = total
+    collect(grads_in, example_sem)
     row = lax.broadcasted_iota(jnp.int32, store_ref.shape, 0)
     store = jnp.zeros(store_ref.shape, jnp.float32)
     for d in range(devices):
-        store = store + jnp.where(row == ids[d], terms[d, rows:2 * rows, :][None], 0.0)
+        store = store + jnp.where(row == ids[d], grads_in[d][None], 0.0)
     store_ref[...] = store * scale
-    for d in range(1, devices):
-        q = me ^ d
-        pltpu.make_async_copy(piece, totals.at[q], tot_sem.at[q]).wait()
+    collect(totals, tot_sem)
     for d in range(devices):
-        fin_ref[d * rows:(d + 1) * rows, :] = totals[d, 0:rows, 0:rank]
-        fout_ref[d * rows:(d + 1) * rows, :] = totals[d, rows:2 * rows, rank:2 * rank]
+        fin_ref[d * rows:(d + 1) * rows, :] = totals[d, :, 0:rank]
+        fout_ref[d * rows:(d + 1) * rows, :] = totals[d, :, rank:2 * rank]
     for copy in copies:
         copy.wait_send()
-    for pair, when in sends:
+    for copy, when in sends:
         if when is None:
-            for copy in pair:
-                copy.wait_send()
+            copy.wait_send()
         else:
-            @pl.when(when)
-            def _():
-                for copy in pair:
-                    copy.wait_send()
+            pl.when(when)(copy.wait_send)
+
+
+def place(store_in, fin_in, fout_in, store_ref, fin_ref, fout_ref):
+    rank = fin_in.shape[0]
+    for q in range(store_in.shape[1]):
+        store_ref[:, q * rank:(q + 1) * rank] = store_in[:, q, 0:rank]
+    fin_ref[...] = fin_in[...]
+    fout_ref[...] = fout_in[...]
 
 
 def fused(hidden_acts, out_grads, proj_in, proj_out, lengths, example_ids):
@@ -205,22 +239,34 @@
             pltpu.VMEM((devices, rank, out_cols), bf16),
             pltpu.VMEM((length, rank), f32),
             pltpu.VMEM((length, rank), f32),
-            pltpu.VMEM((devices, 2 * rows, 2 * rank), f32),
-            pltpu.VMEM((devices, 2 * rows, 2 * rank), f32),
-            pltpu.VMEM((2 * rows, 2 * rank), f32),
-            pltpu.VMEM((devices, 2 * rows, 2 * rank), f32),
-            dma((devices,)), dma((devices,)), dma((2,)), dma((2, 24)),
-            dma((devices,)), dma((devices,)),
-            dma((devices,)), dma((devices,)), dma((devices,)), dma((devices,)),
+            pltpu.VMEM((devices, rows, 2 * rank), f32),
+            pltpu.VMEM((devices, rows, 2 * rank), f32),
+            pltpu.VMEM((devices, rows, 2 * rank), f32),
+            pltpu.VMEM((devices, rows, 2 * rank), f32),
+            pltpu.VMEM((rows, 2 * rank), f32),
+            pltpu.VMEM((devices, rows, 2 * rank), f32),
+            dma((devices,)), dma((devices,)), dma((2,)), dma((96,)),
+            dma((CHUNKS, devices)),
+            dma((devices,)), dma((devices,)), dma((devices,)),
+            dma((devices,)), dma((devices,)), dma((devices,)),
         ],
         compiler_params=pltpu.CompilerParams(
-            collective_id=0, has_side_effects=True, vmem_limit_bytes=40 * 1024 * 1024),
+            collective_id=0, has_side_effects=True, vmem_limit_bytes=58 * 1024 * 1024),
         cost_estimate=pl.CostEstimate(
             flops=2 * length * rank * (ffw + width),
             bytes_accessed=2 * length * (ffw + width), transcendentals=0),
     )(hidden_acts.reshape(length, ffw), out_grads.reshape(length, width),
       proj_in, proj_out, lengths, example_ids)
-    return store[:, :, :rank].reshape(devices, rows * rank), fin, fout
+    return pl.pallas_call(
+        place,
+        out_shape=(
+            jax.ShapeDtypeStruct((devices, rows * rank), f32),
+            jax.ShapeDtypeStruct((rank, rank), f32),
+            jax.ShapeDtypeStruct((rank, rank), f32),
+        ),
+        in_specs=[pl.BlockSpec(memory_space=pltpu.VMEM)] * 3,
+        out_specs=[pl.BlockSpec(memory_space=pltpu.VMEM)] * 3,
+    )(store, fin, fout)
 
 
 def local(hidden_acts, out_grads, proj_in, proj_out, lengths, example_ids):

time: 54.2 us -> 40.4 us (0.75)
  local copies, waits for them, and re-layouts: 10.5 us -> 0 us
  Pallas kernels: 42.7 us -> 39.5 us
    unnamed x14 -> x0, local copies, waits for them, and re-layouts: 9.84 us -> none
    pallas_call x1, Pallas kernels: 42.7 us -> 38 us  [fused(): pl.pallas_call(functools.partial(kernel, 1.0 / math.sqrt(length)), out_sh...]
    pallas_call x0 -> x1, Pallas kernels: none -> 1.48 us  [fused(): pl.pallas_call(place, out_shape=(jax.ShapeDtypeStruct((devices, rows * ra...]
    reshape x1 -> x0, local copies, waits for them, and re-layouts: 0.69 us -> none  [fused(): return (store[:, :, :rank].reshape(devices, rows * rank), fin, fout)]
where the time goes in v2:
time: 40.4 us; the launch traced here: 40.2 us
  Pallas kernels  39.5 us (98%)
  between operations  0.64 us (2%)
    pallas_call x1, Pallas kernels, fused(): pl.pallas_call(functools.partial(kernel, 1.0 / math.sqrt(length)), out_sh...  38 us
    pallas_call x1, Pallas kernels, fused(): pl.pallas_call(place, out_shape=(jax.ShapeDtypeStruct((devices, rows * ra...  1.48 us

profile of v2, /device:TPU:0, one launch (start us, length us, event | category | flops | bytes accessed | tf_op | source)
XLA Modules:
  0.0 40.2 jit_solution(12051376434937162473)
XLA Ops:
  0.6 38.0 %shard_map.85 = (f32[16,4,128]{2,1,0:T(4,128)}, f32[64,64]{1,0:T(8,128)}, f32[64,64]{1,0:T(8,128)}) custom-call(bf16[256,16384]{1,0:T(8,128)(2,1)} %bitcast.2, bf16[256,8192]{1,0:T(8,128)(2,1)} %bitcast.3, bf16[64,1024]{1,0:T(8,128)(2,1)} %pin_hbm.1, bf16[64,512]{1,0:T(8,128)(2,1)} %pout_hbm.1, s32[16]{0:T(128)} %lengths.1, s32[16]{0:T(128)} %ids.1), custom_call_target="tpu_custom_call" | custom-call | flops 805306368 | bytes 12582912 | tf_op jit(solution)/shard_map/pallas_call | solution.py:225
  38.7 1.5 %shard_map.86 = (f32[16,256]{1,0:T(8,128)}, f32[64,64]{1,0:T(8,128)}, f32[64,64]{1,0:T(8,128)}) custom-call(f32[16,4,128]{2,1,0:T(4,128)} %get-tuple-element.6.store_in, f32[64,64]{1,0:T(8,128)} %get-tuple-element.7.fin_in, f32[64,64]{1,0:T(8,128)} %get-tuple-element.8.fout_in), custom_call_target="tpu_custom_call" | custom-call | tf_op jit(solution)/shard_map/pallas_call | solution.py:260
